TPU v7x, 32 devices: a whole 2x2x4 slice. The times are simulated.
32 devices in a mesh: groups: 2 (over y), dom: 4 (over z), sub: 2 (over x), col: 2 (over core).
Axes of the slice: x: 2, y: 2, z: 4, core: 2. Of those that a mesh axis runs over, the one named last changes fastest.
Arguments:
- rhs: float32 [8, 2, 3, 16, 512], P(('groups', 'dom'), 'sub', None, 'col'), parts along dimension 0, may hold values from -200 to 200
- diagonal: float32 [4, 2, 3, 512], P('dom', 'sub'), may hold values from 1 to 3
- lower_vals: float32 [4, 2, 3, 3, 7, 512], P('dom', 'sub'), may hold values from -0.013888889 to 0.013888889
- lower_cols: int32 [4, 2, 7, 512], P('dom', 'sub'), may hold values from 0 to 511, as said below
- face_nodes: int32 [4, 2, 4, 256], P('dom', 'sub'), may hold values from 0 to 511, as said below
- couple: float32 [4, 2, 2, 3, 3, 256], P('dom', 'sub'), may hold values from -0.013888889 to 0.013888889
- face_count: int32 [4, 2, 2], P('dom', 'sub'), may hold values from 64 to 256, as said below
Outputs:
- solution: float32 [8, 2, 3, 16, 512], P(('groups', 'dom'), 'sub', None, 'col'), parts along dimension 0
- residual: float32 [8, 2, 3, 16, 512], P(('groups', 'dom'), 'sub', None, 'col'), parts along dimension 0
There are 2 independent parts, one for each index of `groups`. A program takes and returns all parts, laid end to end along the dimension named above; an argument that names none is the same for every part. Nothing has to cross between parts.
Inputs may be any that keep to these rules, and one draw needn't show every extreme that they name: `lower_cols`: for every partition and slot, the row of 512 entries is a permutation of the local nodes. `face_nodes`: each of the four lists of a partition names 256 different local nodes. `face_count`: some pair of each kind has all 256 slots live.
All inputs are finite; a program needn't handle non-finite values.
Results may differ from a plain program's by a relative error of at most 0.0003.
Values sent between devices are 32-bit elements; how exact they have to be, the bound alone decides.
A program may use at most 128 MiB of HBM per device.

v0:
```python
import jax
import jax.numpy as jnp
from jax import lax
from jax.sharding import PartitionSpec as P

ITERS = 2


def shifted(value, axis, steps):
    count = lax.axis_size(axis)
    first, last = (max(0, -steps), min(count, count - steps))
    return lax.ppermute(value, axis, [(source, source + steps) for source in range(first, last)])


def local_apply(field, diagonal_part, blocks, index, inverse):
    highest = lax.Precision.HIGHEST
    result = diagonal_part[:, None, :] * field
    near = field[:, :, index]
    result = result + jnp.einsum("abkn,bckn->acn", blocks, near, precision=highest)
    back = jnp.einsum("abkn,acn->bckn", blocks, field, precision=highest)
    returned = jnp.take_along_axis(back, inverse[None, None, :, :], axis=3)
    return result + jnp.sum(returned, axis=2)


def cholesky_solve(matrix, right):
    order = matrix.shape[0]
    factor = jnp.zeros_like(matrix)
    for j in range(order):
        pivot = jnp.sqrt(matrix[j, j] - jnp.sum(factor[j, :j] * factor[j, :j]))
        factor = factor.at[j, j].set(pivot)
        if j + 1 < order:
            below = matrix[j + 1 :, j] - jnp.sum(
                factor[j + 1 :, :j] * factor[j, :j][None, :], axis=1
            )
            factor = factor.at[j + 1 :, j].set(below / pivot)
    middle = []
    for j in range(order):
        value = right[j]
        for k in range(j):
            value = value - factor[j, k] * middle[k]
        middle.append(value / factor[j, j])
    answer = [None] * order
    for j in range(order - 1, -1, -1):
        value = middle[j]
        for k in range(j + 1, order):
            value = value - factor[k, j] * answer[k]
        answer[j] = value / factor[j, j]
    return jnp.stack(answer, axis=0)


def body(rhs, diagonal, lower_vals, lower_cols, face_nodes, couple, face_count):
    highest = lax.Precision.HIGHEST
    start = rhs[0, 0]
    width = start.shape[1]
    total = width * lax.axis_size("col")
    offset = lax.axis_index("col") * width
    diagonal_part = diagonal[0, 0]
    blocks = lower_vals[0, 0]
    index = lower_cols[0, 0]
    slot_rows = lax.broadcasted_iota(jnp.int32, index.shape, 0)
    node_ids = lax.broadcasted_iota(jnp.int32, index.shape, 1)
    inverse = jnp.zeros_like(index).at[slot_rows, index].set(node_ids)
    faces = face_nodes[0, 0]
    slots = lax.broadcasted_iota(jnp.int32, (couple.shape[-1],), 0)
    live = (slots[None, :] < face_count[0, 0][:, None]).astype(jnp.float32)
    weights = couple[0, 0] * live[:, None, None, :]

    def gram_block(left, right):
        block = jnp.einsum("acn,adn->cd", left, right, precision=highest)
        return lax.dynamic_update_slice(jnp.zeros((total, total), jnp.float32), block, (0, offset))

    def mixing(whole, coefficients):
        columns = lax.dynamic_slice_in_dim(coefficients, offset, width, 1)
        return jnp.einsum("acn,cd->adn", whole, columns, precision=highest)

    whole_start = lax.all_gather(start, "col", axis=1, tiled=True)
    norms = lax.psum(gram_block(whole_start, start), ("dom", "sub", "col"))
    solution = jnp.zeros_like(start)
    residual = start
    directions = whole_start
    for iteration in range(ITERS):
        field = lax.dynamic_slice_in_dim(directions, offset, width, 1)
        result = local_apply(field, diagonal_part, blocks, index, inverse)
        dom_weights = weights[0]
        sent = jnp.einsum("abk,ack->bck", dom_weights, field[:, :, faces[1]], precision=highest)
        result = result.at[:, :, faces[0]].add(shifted(sent, "dom", 1))
        arrived = shifted(field[:, :, faces[0]], "dom", -1)
        result = result.at[:, :, faces[1]].add(
            jnp.einsum("abk,bck->ack", dom_weights, arrived, precision=highest)
        )
        sub_weights = weights[1]
        sent = jnp.einsum("abk,ack->bck", sub_weights, field[:, :, faces[3]], precision=highest)
        result = result.at[:, :, faces[2]].add(shifted(sent, "sub", 1))
        arrived = shifted(field[:, :, faces[2]], "sub", -1)
        result = result.at[:, :, faces[3]].add(
            jnp.einsum("abk,bck->ack", sub_weights, arrived, precision=highest)
        )
        images = lax.all_gather(result, "col", axis=1, tiled=True)
        curvature = lax.psum(gram_block(directions, result), ("dom", "sub", "col"))
        alpha = cholesky_solve(curvature, norms)
        solution = solution + mixing(directions, alpha)
        residual = residual - mixing(images, alpha)
        if iteration + 1 < ITERS:
            whole_residual = lax.all_gather(residual, "col", axis=1, tiled=True)
            fresh = lax.psum(gram_block(whole_residual, residual), ("dom", "sub", "col"))
            beta = cholesky_solve(norms, fresh)
            directions = whole_residual + jnp.einsum(
                "acn,cd->adn", directions, beta, precision=highest
            )
            norms = fresh
    return (solution[None, None], residual[None, None])


def solution(mesh):
    placed = (
        P(("groups", "dom"), "sub", None, "col", None),
        P("dom", "sub", None, None),
        P("dom", "sub", None, None, None, None),
        P("dom", "sub", None, None),
        P("dom", "sub", None, None),
        P("dom", "sub", None, None, None, None),
        P("dom", "sub", None),
    )
    return jax.shard_map(
        body,
        mesh=mesh,
        in_specs=placed,
        out_specs=(
            P(("groups", "dom"), "sub", None, "col", None),
            P(("groups", "dom"), "sub", None, "col", None),
        ),
        check_vma=False,
    )
```

profile of v0, /device:TPU:0, one launch (start us, length us, event | category | flops | bytes accessed | tf_op | source)
XLA Modules:
  0.0 1644.9 jit_solution(111502192944585266)
XLA Ops:
  32.8 13.7 scatter_custom_fusion.8
  60.9 16.5 %copy.329 = f32[3,8,7,512]{1,0,3,2:T(4,128)} copy(f32[3,8,7,512]{2,1,0,3:T(8,128)} %fusion.10) | data formatting | bytes 688128 | tf_op jit(solution)/shard_map/abkn,acn->bckn/transpose | solution.py:20
  77.4 35.4 %gather_fusion.10 = f32[3584,3,8]{2,1,0:T(4,128)} fusion(f32[3,8,7,512]{1,0,3,2:T(4,128)} %copy.329, s32[3584]{0:T(1024)S(1)} %reshape.2882), kind=kCustom, calls=%fused_computation.clone | custom fusion | bytes 716800 | tf_op jit(solution)/shard_map/jit(take_along_axis)/gather | solution.py:21
  121.9 13.5 gather_fusion
  148.1 14.4 fusion.16
  169.9 26.3 %scatter_fusion = f32[3,8,512]{1,0,2:T(4,128)} fusion(f32[3,8,512]{1,0,2:T(4,128)} %copy.333, s32[256]{0:T(256)S(1)} %bitcast.1550, f32[256,3,8]{2,1,0:T(4,128)} %bitcast.25), kind=kCustom, calls=%fused_computation.12 | custom fusion | flops 6144 | bytes 74752 | tf_op jit(solution)/shard_map/scatter-add | solution.py:86
  196.3 26.3 %scatter_fusion.1 = f32[3,8,512]{1,0,2:T(4,128)} fusion(f32[3,8,512]{1,0,2:T(4,128)} %scatter_fusion, s32[256]{0:T(256)S(1)} %bitcast.1547, f32[256,3,8]{2,1,0:T(4,128)} %fusion.36), kind=kCustom, calls=%fused_computation.13 | custom fusion | flops 6144 | bytes 74752 | tf_op jit(solution)/shard_map/scatter-add | solution.py:88
  222.6 26.3 %scatter_fusion.2 = f32[3,8,512]{1,0,2:T(4,128)} fusion(f32[3,8,512]{1,0,2:T(4,128)} %scatter_fusion.1, s32[256]{0:T(256)S(1)} %bitcast.1544, f32[256,3,8]{2,1,0:T(4,128)} %bitcast.34), kind=kCustom, calls=%fused_computation.14 | custom fusion | flops 6144 | bytes 74752 | tf_op jit(solution)/shard_map/scatter-add | solution.py:93
  253.2 26.5 %scatter_fusion.3 = f32[3,8,512]{1,0,2:T(4,128)} fusion(f32[3,8,512]{1,0,2:T(4,128)} %scatter_fusion.2, s32[256]{0:T(256)S(1)} %bitcast.1541, f32[256,3,8]{2,1,0:T(4,128)} %fusion.38), kind=kCustom, calls=%fused_computation.15 | custom fusion | flops 6144 | bytes 74752 | tf_op jit(solution)/shard_map/scatter-add | solution.py:95
  281.6 63.8 %all-reduce.3 = (f32[16,16]{1,0:T(8,128)S(1)}, f32[16,16]{1,0:T(8,128)S(1)}) all-reduce(f32[16,16]{1,0:T(8,128)S(1)} %dynamic_update_slice.12, f32[16,16]{1,0:T(8,128)S(1)} %dynamic_update_slice.13), channel_id=1, replica_groups=mesh['groups'=2,'dom'=4,'sub'=2,'col'=2] {'dom','sub','col'}, use_global_device_ids=true, to_apply=%region_0.0 | all-reduce | flops 512 | bytes 4096 | tf_op jit(solution)/shard_map/psum | solution.py:77
  443.3 74.3 %subtract_divide_fusion.118 = (f32[1,16]{1,0:T(1,128)S(1)}, f32[1,16]{1,0:T(1,128)S(1)}, f32[1,16]{1,0:T(1,128)S(1)}, f32[1,16]{1,0:T(1,128)S(1)}, f32[1,16]{1,0...) fusion(f32[16,16]{1,0:T(8,128)S(1)} %get-tuple-element.1125, ...), kind=kLoop, calls=%fused_computation.727 | loop fusion | flops 3600 | bytes 2400 | tf_op jit(solution)/shard_map/div | solution.py:41
  517.6 73.6 %subtract_divide_fusion.147 = (f32[16]{0:T(128)S(1)}, f32[16]{0:T(128)S(1)}, f32[16]{0:T(128)S(1)}, f32[16]{0:T(128)S(1)}, f32[16]{0:T(128)S(1)}, /*index=5*/f32...) fusion(f32[1,16]{1,0:T(1,128)S(1)} %get-tuple-element.1270, ...), kind=kLoop, calls=%fused_computation.757 | loop fusion | flops 3584 | bytes 2332 | tf_op jit(solution)/shard_map/div | solution.py:41
  592.5 57.1 %subtract_divide_fusion.134 = (f32[16]{0:T(128)S(1)}, f32[16]{0:T(128)S(1)}, f32[16]{0:T(128)S(1)}, f32[16]{0:T(128)S(1)}, f32[16]{0:T(128)S(1)}, /*index=5*/f32...) fusion(f32[16]{0:T(128)S(1)} %get-tuple-element.1298, ...), kind=kLoop, calls=%fused_computation.744 | loop fusion | flops 3184 | bytes 2232 | tf_op jit(solution)/shard_map/div | solution.py:47
  649.6 27.7 %divide_bitcast_fusion.2 = (f32[1,16]{1,0:T(1,128)S(1)}, f32[16]{0:T(128)S(1)}, f32[16]{0:T(128)S(1)}) fusion(f32[16]{0:T(128)S(1)} %get-tuple-element.1286, f32[16]{0:T(128)S(1)} %get-tuple-element.1285, f32[16]{0:T(128)S(1)} %get-tuple-element.1284, f32[16]{0:T(128)S(1)} %get-tuple-element.1283, f32[16]{0:T(128)S(1)} %get-tuple-element.1282, ...), kind=kLoop, calls=%fused_computation.741 | loop fusion | flops 1392 | bytes 1396 | tf_op jit(solution)/shard_map/stack | solution.py:48
  677.3 57.1 %subtract_divide_fusion.105 = (f32[1,16]{1,0:T(1,128)S(1)}, f32[1,16]{1,0:T(1,128)S(1)}, f32[1,16]{1,0:T(1,128)S(1)}, f32[1,16]{1,0:T(1,128)S(1)}, f32[1,16]{1,0...) fusion(f32[1,16]{1,0:T(1,128)S(1)} %get-tuple-element.1267, ...), kind=kLoop, calls=%fused_computation.714 | loop fusion | flops 3184 | bytes 2232 | tf_op jit(solution)/shard_map/div | solution.py:47
  738.3 30.2 %psum.30 = f32[16,16]{1,0:T(8,128)S(1)} all-reduce(f32[16,16]{1,0:T(8,128)S(1)} %dynamic_update_slice.14), channel_id=1, replica_groups=mesh['groups'=2,'dom'=4,'sub'=2,'col'=2] {'dom','sub','col'}, use_global_device_ids=true, to_apply=%region_35.0 | all-reduce | flops 256 | bytes 2048 | tf_op jit(solution)/shard_map/psum | solution.py:105
  768.5 75.6 %subtract_divide_fusion.66 = (f32[1,16]{1,0:T(1,128)S(1)}, f32[1,16]{1,0:T(1,128)S(1)}, f32[1,16]{1,0:T(1,128)S(1)}, f32[1,16]{1,0:T(1,128)S(1)}, f32[1,16]{1,0:...) fusion(f32[]{:T(128)} %bitcast.445, ...), kind=kLoop, calls=%fused_computation.674 | loop fusion | flops 3600 | bytes 2400 | tf_op jit(solution)/shard_map/div | solution.py:41
  844.1 75.5 %subtract_divide_fusion.95 = (f32[16]{0:T(128)}, f32[16]{0:T(128)}, f32[16]{0:T(128)}, f32[16]{0:T(128)}, f32[16]{0:T(128)}, /*index=5*/f32[16]{0:T(128)}, f32[1...) fusion(f32[1,16]{1,0:T(1,128)S(1)} %get-tuple-element.1212, ...), kind=kLoop, calls=%fused_computation.704 | loop fusion | flops 3584 | bytes 2332 | tf_op jit(solution)/shard_map/div | solution.py:41
  920.9 58.8 %subtract_divide_fusion.82 = (f32[16]{0:T(128)S(1)}, f32[16]{0:T(128)S(1)}, f32[16]{0:T(128)S(1)}, f32[16]{0:T(128)S(1)}, f32[16]{0:T(128)S(1)}, /*index=5*/f32[...) fusion(f32[16]{0:T(128)} %get-tuple-element.1240, ...), kind=kLoop, calls=%fused_computation.691 | loop fusion | flops 3184 | bytes 2232 | tf_op jit(solution)/shard_map/div | solution.py:47
  979.7 28.9 %divide_bitcast_fusion.1 = (f32[1,16]{1,0:T(1,128)}, f32[16]{0:T(128)}, f32[16]{0:T(128)}) fusion(f32[16]{0:T(128)S(1)} %get-tuple-element.1228, f32[16]{0:T(128)S(1)} %get-tuple-element.1227, f32[16]{0:T(128)S(1)} %get-tuple-element.1226, f32[16]{0:T(128)S(1)} %get-tuple-element.1225, f32[16]{0:T(128)S(1)} %get-tuple-element.1224, ...), kind=kLoop, calls=%fused_computation.688 | loop fusion | flops 1392 | bytes 1396 | tf_op jit(solution)/shard_map/stack | solution.py:48
  1008.6 58.5 %subtract_divide_fusion.53 = (f32[1,16]{1,0:T(1,128)S(1)}, f32[1,16]{1,0:T(1,128)S(1)}, f32[1,16]{1,0:T(1,128)S(1)}, f32[1,16]{1,0:T(1,128)S(1)}, f32[1,16]{1,0:...) fusion(f32[1,16]{1,0:T(1,128)S(1)} %get-tuple-element.1209, ...), kind=kLoop, calls=%fused_computation.661 | loop fusion | flops 3184 | bytes 2232 | tf_op jit(solution)/shard_map/div | solution.py:47
  1072.0 14.0 gather_fusion.5
  1111.3 16.6 %copy.376 = f32[3,8,7,512]{1,0,3,2:T(4,128)} copy(f32[3,8,7,512]{2,1,0,3:T(8,128)} %fusion.13) | data formatting | bytes 688128 | tf_op jit(solution)/shard_map/abkn,acn->bckn/transpose | solution.py:20
  1127.9 35.4 %gather_fusion.11 = f32[3584,3,8]{2,1,0:T(4,128)} fusion(f32[3,8,7,512]{1,0,3,2:T(4,128)} %copy.376, s32[3584]{0:T(1024)S(1)} %reshape.2882), kind=kCustom, calls=%fused_computation.1.clone | custom fusion | bytes 716800 | tf_op jit(solution)/shard_map/jit(take_along_axis)/gather | solution.py:21
  1184.6 14.4 fusion.21
  1224.0 16.9 %scatter_fusion.4 = f32[3,8,512]{1,0,2:T(4,128)S(1)} fusion(f32[3,8,512]{1,0,2:T(4,128)S(1)} %copy.379, s32[256]{0:T(256)S(1)} %bitcast.1551, f32[256,3,8]{2,1,0:T(4,128)} %bitcast.1537), kind=kCustom, calls=%fused_computation.16 | custom fusion | flops 6144 | bytes 74752 | tf_op jit(solution)/shard_map/scatter-add | solution.py:86
  1270.0 30.0 %psum.31 = f32[16,16]{1,0:T(8,128)S(1)} all-reduce(f32[16,16]{1,0:T(8,128)S(1)} %dynamic_update_slice.15), channel_id=1, replica_groups=mesh['groups'=2,'dom'=4,'sub'=2,'col'=2] {'dom','sub','col'}, use_global_device_ids=true, to_apply=%region_68.0 | all-reduce | flops 256 | bytes 2048 | tf_op jit(solution)/shard_map/psum | solution.py:99
  1349.3 74.9 %subtract_divide_fusion.13 = (f32[1,16]{1,0:T(1,128)S(1)}, f32[1,16]{1,0:T(1,128)S(1)}, f32[1,16]{1,0:T(1,128)S(1)}, f32[1,16]{1,0:T(1,128)S(1)}, f32[1,16]{1,0:...) fusion(f32[]{:T(128)} %bitcast.665, ...), kind=kLoop, calls=%fused_computation.620 | loop fusion | flops 3600 | bytes 2400 | tf_op jit(solution)/shard_map/div | solution.py:41
  1424.2 74.2 %subtract_divide_fusion.42 = (f32[16]{0:T(128)S(1)}, f32[16]{0:T(128)S(1)}, f32[16]{0:T(128)S(1)}, f32[16]{0:T(128)S(1)}, f32[16]{0:T(128)S(1)}, /*index=5*/f32[...) fusion(f32[1,16]{1,0:T(1,128)S(1)} %get-tuple-element.1154, ...), kind=kLoop, calls=%fused_computation.650 | loop fusion | flops 3584 | bytes 2332 | tf_op jit(solution)/shard_map/div | solution.py:41
  1499.6 57.5 %subtract_divide_fusion.29 = (f32[16]{0:T(128)S(1)}, f32[16]{0:T(128)S(1)}, f32[16]{0:T(128)S(1)}, f32[16]{0:T(128)S(1)}, f32[16]{0:T(128)S(1)}, /*index=5*/f32[...) fusion(f32[16]{0:T(128)S(1)} %get-tuple-element.1182, ...), kind=kLoop, calls=%fused_computation.637 | loop fusion | flops 3184 | bytes 2232 | tf_op jit(solution)/shard_map/div | solution.py:47
  1557.1 28.0 %divide_bitcast_fusion = (f32[1,16]{1,0:T(1,128)S(1)}, f32[16]{0:T(128)S(1)}, f32[16]{0:T(128)S(1)}) fusion(f32[16]{0:T(128)S(1)} %get-tuple-element.1170, f32[16]{0:T(128)S(1)} %get-tuple-element.1169, f32[16]{0:T(128)S(1)} %get-tuple-element.1168, f32[16]{0:T(128)S(1)} %get-tuple-element.1167, f32[16]{0:T(128)S(1)} %get-tuple-element.1166, ...), kind=kLoop, calls=%fused_computation.634 | loop fusion | flops 1392 | bytes 1396 | tf_op jit(solution)/shard_map/stack | solution.py:48
  1585.1 57.5 %subtract_divide_fusion = (f32[1,16]{1,0:T(1,128)S(1)}, f32[1,16]{1,0:T(1,128)S(1)}, f32[1,16]{1,0:T(1,128)S(1)}, f32[1,16]{1,0:T(1,128)S(1)}, f32[1,16]{1,0:T(1...) fusion(f32[1,16]{1,0:T(1,128)S(1)} %get-tuple-element.1151, ...), kind=kLoop, calls=%fused_computation.607 | loop fusion | flops 3184 | bytes 2232 | tf_op jit(solution)/shard_map/div | solution.py:47
  (483 shorter events, 276.9 us)
Async XLA Ops:
  3.4 25.9 %copy-start.2 = (f32[3,8,512]{1,0,2:T(4,128)}, f32[3,8,512]{1,0,2:T(4,128)S(1)}, u32[]{:S(2)}) copy-start(f32[3,8,512]{1,0,2:T(4,128)S(1)} %copy.323) | copy-start | bytes 147460
  4.3 165.6 %copy-start.20 = (s32[256,1]{0,1:T(1,128)}, s32[256,1]{0,1:T(1,128)S(1)}, u32[]{:S(2)}) copy-start(s32[256,1]{0,1:T(1,128)S(1)} %get-tuple-element.1760) | copy-start | bytes 3076
  4.3 192.0 %copy-start.18 = (s32[256,1]{0,1:T(1,128)}, s32[256,1]{0,1:T(1,128)S(1)}, u32[]{:S(2)}) copy-start(s32[256,1]{0,1:T(1,128)S(1)} %get-tuple-element.1759) | copy-start | bytes 3076
  4.3 218.3 %copy-start.16 = (s32[256,1]{0,1:T(1,128)}, s32[256,1]{0,1:T(1,128)S(1)}, u32[]{:S(2)}) copy-start(s32[256,1]{0,1:T(1,128)S(1)} %get-tuple-element.1761) | copy-start | bytes 3076
  4.3 248.9 %copy-start.14 = (s32[256,1]{0,1:T(1,128)}, s32[256,1]{0,1:T(1,128)S(1)}, u32[]{:S(2)}) copy-start(s32[256,1]{0,1:T(1,128)S(1)} %get-tuple-element.1758) | copy-start | bytes 3076
  4.4 28.0 %copy-start.22 = (s32[1,1,7,512]{3,1,2,0:T(1,128)S(1)}, s32[1,1,7,512]{3,1,2,0:T(1,128)}, u32[]{:S(2)}) copy-start(s32[1,1,7,512]{3,1,2,0:T(1,128)} %param.198) | copy-start | bytes 43012
  4.4 28.1 %copy-start.29 = (s32[2]{0:T(128)S(1)}, s32[2]{0:T(128)}, u32[]{:S(2)}) copy-start(s32[2]{0:T(128)} %constant.2001) | copy-start | bytes 28
  4.4 28.2 %copy-start.28 = (s32[2]{0:T(128)S(1)}, s32[2]{0:T(128)}, u32[]{:S(2)}) copy-start(s32[2]{0:T(128)} %constant.1998) | copy-start | bytes 28
  8.0 39.8 %copy-start.9 = (f32[1,1,3,3,7,512]{5,1,4,3,2,0:T(1,128)S(1)}, f32[1,1,3,3,7,512]{5,1,4,3,2,0:T(1,128)}, u32[]{:S(2)}) copy-start(f32[1,1,3,3,7,512]{5,1,4,3,2,0:T(1,128)} %param.197) | copy-start | bytes 387076
  8.6 37.9 %copy-start = (f32[2,3,3,256]{1,2,3,0:T(4,128)}, f32[2,3,3,256]{1,2,3,0:T(4,128)S(1)}, u32[]{:S(2)}) copy-start(f32[2,3,3,256]{1,2,3,0:T(4,128)S(1)} %bitcast_multiply_fusion) | copy-start | bytes 55300
  12.7 157.2 %collective-permute-start = (f32[3,8,256]{1,0,2:T(4,128)}, f32[3,8,256]{1,0,2:T(4,128)}, u32[]{:S(2)}, u32[]{:S(2)}) collective-permute-start(f32[3,8,256]{1,0,2:T(4,128)} %convolution_bitcast_fusion.3), channel_id=1, source_target_pairs={{0,4},{4,8},{8,12},{1,5},{5,9},{9,13},{2,6},{6,10},{10,14},{3,7},{... | collective-permute-start | bytes 73736 | tf_op jit(solution)/shard_map/ppermute | solution.py:12
  18.3 14.1 copy-start.24
  20.1 145.6 %collective-permute-start.1 = (f32[3,8,256]{1,0,2:T(4,128)}, f32[3,8,256]{1,0,2:T(4,128)}, u32[]{:S(2)}, u32[]{:S(2)}) collective-permute-start(f32[3,8,256]{1,0,2:T(4,128)} %bitcast.26), channel_id=1, source_target_pairs={{4,0},{8,4},{12,8},{5,1},{9,5},{13,9},{6,2},{10,6},{14,10},{7,3},{... | collective-permute-start | bytes 73736 | tf_op jit(solution)/shard_map/ppermute | solution.py:12
  25.1 197.6 %collective-permute-start.2 = (f32[3,8,256]{1,0,2:T(4,128)}, f32[3,8,256]{1,0,2:T(4,128)}, u32[]{:S(2)}, u32[]{:S(2)}) collective-permute-start(f32[3,8,256]{1,0,2:T(4,128)} %convolution_bitcast_fusion.2), channel_id=1, source_target_pairs={{0,2},{1,3},{4,6},{5,7},{8,10},{9,11},{12,14},{13,15},{16,18},{17,... | collective-permute-start | bytes 73736 | tf_op jit(solution)/shard_map/ppermute | solution.py:12
  31.1 217.9 %collective-permute-start.3 = (f32[3,8,256]{1,0,2:T(4,128)}, f32[3,8,256]{1,0,2:T(4,128)}, u32[]{:S(2)}, u32[]{:S(2)}) collective-permute-start(f32[3,8,256]{1,0,2:T(4,128)} %bitcast.35), channel_id=1, source_target_pairs={{2,0},{3,1},{6,4},{7,5},{10,8},{11,9},{14,12},{15,13},{18,16},{19,... | collective-permute-start | bytes 73736 | tf_op jit(solution)/shard_map/ppermute | solution.py:12
  46.5 66.3 %copy-start.12 = (pred[7,512]{1,0:T(8,128)(4,1)}, pred[7,512]{1,0:T(8,128)(4,1)S(1)}, u32[]{:S(2)}) copy-start(pred[7,512]{1,0:T(8,128)(4,1)S(1)} %and_bitcast_fusion) | copy-start | bytes 10756
  121.8 26.2 %copy-start.8 = (s32[4096]{0:T(1024)}, s32[4096]{0:T(1024)S(1)}, u32[]{:S(2)}) copy-start(s32[4096]{0:T(1024)S(1)} %pad_clamp_fusion) | copy-start | bytes 49156
  148.1 15.9 copy-start.27
  148.1 15.9 copy-start.5
  164.0 58.6 %copy-start.10 = (f32[1,1,3,512]{3,2,1,0:T(4,128)}, f32[1,1,3,512]{3,2,1,0:T(4,128)S(1)}, u32[]{:S(2)}) copy-start(f32[1,1,3,512]{3,2,1,0:T(4,128)S(1)} %copy.435) | copy-start | bytes 18436
  768.5 298.6 %copy-start.6 = (f32[16,16]{1,0:T(8,128)}, f32[16,16]{1,0:T(8,128)S(1)}, u32[]{:S(2)}) copy-start(f32[16,16]{1,0:T(8,128)S(1)} %psum.30) | copy-start | bytes 3076
  1111.3 52.0 %copy-start.13 = (pred[7,512]{1,0:T(8,128)(4,1)S(1)}, pred[7,512]{1,0:T(8,128)(4,1)}, u32[]{:S(2)}) copy-start(pred[7,512]{1,0:T(8,128)(4,1)} %copy-done.12) | copy-start | bytes 10756
  1184.6 16.0 copy-start.11
  1200.6 23.4 %copy-start.21 = (s32[256,1]{0,1:T(1,128)S(1)}, s32[256,1]{0,1:T(1,128)}, u32[]{:S(2)}) copy-start(s32[256,1]{0,1:T(1,128)} %copy-done.20) | copy-start | bytes 3076
  1204.1 19.1 %collective-permute-start.4 = (f32[3,8,256]{1,0,2:T(4,128)S(1)}, f32[3,8,256]{1,0,2:T(4,128)S(1)}, u32[]{:S(2)}, u32[]{:S(2)}) collective-permute-start(f32[3,8,256]{1,0,2:T(4,128)S(1)} %convolution_bitcast_fusion.1), channel_id=1, source_target_pairs={{0,4},{4,8},{8,12},{1,5},{5,9},{9,13},{2,6},{6,10},{10,14},{3,7},{... | collective-permute-start | bytes 73736 | tf_op jit(solution)/shard_map/ppermute | solution.py:12
  1205.4 35.5 %copy-start.19 = (s32[256,1]{0,1:T(1,128)S(1)}, s32[256,1]{0,1:T(1,128)}, u32[]{:S(2)}) copy-start(s32[256,1]{0,1:T(1,128)} %copy-done.18) | copy-start | bytes 3076
  1205.4 15.6 collective-permute-start.5
  1209.4 39.9 %collective-permute-start.6 = (f32[3,8,256]{1,0,2:T(4,128)}, f32[3,8,256]{1,0,2:T(4,128)S(1)}, u32[]{:S(2)}, u32[]{:S(2)}) collective-permute-start(f32[3,8,256]{1,0,2:T(4,128)} %convolution_bitcast_fusion), channel_id=1, source_target_pairs={{0,2},{1,3},{4,6},{5,7},{8,10},{9,11},{12,14},{13,15},{16,18},{17,... | collective-permute-start | bytes 73736 | tf_op jit(solution)/shard_map/ppermute | solution.py:12
  1210.7 46.9 %collective-permute-start.7 = (f32[3,8,256]{1,0,2:T(4,128)}, f32[3,8,256]{1,0,2:T(4,128)}, u32[]{:S(2)}, u32[]{:S(2)}) collective-permute-start(f32[3,8,256]{1,0,2:T(4,128)} %bitcast.1591), channel_id=1, source_target_pairs={{2,0},{3,1},{6,4},{7,5},{10,8},{11,9},{14,12},{15,13},{18,16},{19,... | collective-permute-start | bytes 73736 | tf_op jit(solution)/shard_map/ppermute | solution.py:12
  1224.0 25.3 %copy-start.17 = (s32[256,1]{0,1:T(1,128)S(1)}, s32[256,1]{0,1:T(1,128)}, u32[]{:S(2)}) copy-start(s32[256,1]{0,1:T(1,128)} %copy-done.16) | copy-start | bytes 3076
  1249.3 11.6 copy-start.15
  1260.9 88.4 %copy-start.7 = (f32[16,16]{1,0:T(8,128)S(1)}, f32[16,16]{1,0:T(8,128)}, u32[]{:S(2)}) copy-start(f32[16,16]{1,0:T(8,128)} %copy-done.6) | copy-start | bytes 3076
  (6 other events, 32.4 us)
where the time goes:
time: 1670 us; the launch traced here: 1640 us
  other arithmetic  1080 us (65%)
  local copies, waits for them, and re-layouts  253 us (15%)
  blocking collectives  132 us (8%)
  matrix products  83.1 us (5%)
  between operations  68.7 us (4%)
  starting transfers between devices  17.8 us (1%)
    div x6, other arithmetic, cholesky_solve(): middle.append(value / factor[j, j])  448 us
    div x6, other arithmetic, cholesky_solve(): answer[j] = value / factor[j, j]  346 us
    another operation x3, other arithmetic, cholesky_solve(): return jnp.stack(answer, axis=0)  84.6 us
    gather x3, local copies, waits for them, and re-layouts, local_apply(): returned = jnp.take_along_axis(back, inverse[None, None, :, :], axis=3)  70.8 us
    psum x1, blocking collectives, body(): norms = lax.psum(gram_block(whole_start, start), ('dom', 'sub', 'col'))  63.8 us
    gather x4, local copies, waits for them, and re-layouts, local_apply(): near = field[:, :, index]  52.5 us
    scatter-add x2, other arithmetic, body(): result = result.at[:, :, faces[0]].add(shifted(sent, 'dom', 1))  43.3 us
    scatter-add x2, other arithmetic, body(): result.at[:, :, faces[3]]  34.8 us
  transfers between devices with their start and end apart: 8, of which 1 were waited for; matrix products, arithmetic and copies ran while one was open for 16% of the time, Pallas kernels for 0%

commit v1 on v0

v1 whole, which is shorter than its diff:
```python
import functools

import jax
import jax.numpy as jnp
from jax import lax
from jax.experimental import pallas as pl
from jax.experimental.pallas import tpu as pltpu
from jax.sharding import PartitionSpec as P

MESH = pl.DeviceIdType.MESH
SHIFT = 2.0
HIGHEST = lax.Precision.HIGHEST
F32 = jnp.float32


def dot(left, right, dims, precision=None):
    return lax.dot_general(left, right, (dims, ((), ())), precision=precision, preferred_element_type=F32)


NN = ((1,), (0,))
NT = ((1,), (1,))
TN = ((0,), (0,))


def halves(value):
    high = value.astype(jnp.bfloat16).astype(F32)
    return jnp.concatenate([high, value - high], axis=0).astype(jnp.bfloat16)


def joined(value):
    rows = value.shape[0] // 2
    return value[:rows] + value[rows:]


def eliminate(matrix, right):
    order = matrix.shape[0]
    lanes = right.shape[1]
    row = lax.broadcasted_iota(jnp.int32, (order, lanes), 0)
    columns = [jnp.broadcast_to(matrix[:, j : j + 1], (order, lanes)) for j in range(order)]
    scale = jnp.zeros((order, lanes), F32)
    for k in range(order):
        inverse = 1.0 / columns[k][k : k + 1, :]
        scale = jnp.where(row == k, inverse, scale)
        factor = jnp.where(row == k, 0.0, columns[k] * inverse)
        for j in range(k + 1, order):
            columns[j] = columns[j] - factor * columns[j][k : k + 1, :]
        right = right - factor * right[k : k + 1, :]
    return right * scale


def kernel(
    n_dom, n_sub, n_col,
    rhs_ref, diag_ref, vals_ref, cols_ref, faces_ref, couple_ref, count_ref,
    sol_ref, res_ref,
    pick, basis, out_halo, in_halo, weights, message, stage_dom, stage_rest,
    halo_send, halo_recv, col_send, col_recv, dom_send, dom_recv, rest_send, rest_recv,
):
    dom = lax.axis_index("dom")
    sub = lax.axis_index("sub")
    col = lax.axis_index("col")
    width = rhs_ref.shape[1]
    node = rhs_ref.shape[2]
    slots = cols_ref.shape[0]
    iface = faces_ref.shape[1]
    inner = slots * node
    total = width * n_col
    rest = sub * n_col + col
    n_rest = n_sub * n_col

    barrier = pltpu.get_barrier_semaphore()
    for k in range(1, n_dom):
        pl.semaphore_signal(barrier, inc=1, device_id={"dom": lax.rem(dom + k, n_dom)}, device_id_type=MESH)
    for k in range(1, n_rest):
        peer = lax.rem(rest + k, n_rest)
        pl.semaphore_signal(
            barrier, inc=1, device_id={"sub": lax.div(peer, n_col), "col": lax.rem(peer, n_col)}, device_id_type=MESH
        )

    slab = 32

    def build_faces(i, _):
        rows = pl.ds(pl.multiple_of(i * slab, slab), slab)
        ids = lax.broadcasted_iota(jnp.int32, (slab, iface), 0) + i * slab
        for f in range(4):
            hit = ids == faces_ref[f : f + 1, :]
            pick[rows, inner + f * iface : inner + (f + 1) * iface] = jnp.where(hit, 1.0, 0.0).astype(jnp.bfloat16)
        return 0

    def build_inner(i, _):
        rows = pl.ds(pl.multiple_of(i * slab, slab), slab)
        ids = lax.broadcasted_iota(jnp.int32, (slab, node), 0) + i * slab
        for s in range(slots):
            hit = ids == cols_ref[s : s + 1, :]
            pick[rows, s * node : (s + 1) * node] = jnp.where(hit, 1.0, 0.0).astype(jnp.bfloat16)
        return 0

    lax.fori_loop(0, node // slab, build_faces, 0)
    lane = lax.broadcasted_iota(jnp.int32, (3, iface), 1)
    for t in range(2):
        for a in range(3):
            weights[t, a] = jnp.where(lane < count_ref[t], couple_ref[t, a], 0.0)

    basis[0, col] = rhs_ref[...]
    for t in range(2):
        for it in range(2):

            @pl.when((dom == 0) if t == 0 else (sub == 0))
            def _():
                in_halo[it, 2 * t] = jnp.zeros((3 * width, iface), F32)

            @pl.when((dom == n_dom - 1) if t == 0 else (sub == n_sub - 1))
            def _():
                in_halo[it, 2 * t + 1] = jnp.zeros((3 * width, iface), F32)

    pl.semaphore_wait(barrier, n_dom - 1 + n_rest - 1)

    def col_copy(v):
        return pltpu.make_async_remote_copy(
            src_ref=basis.at[v, col], dst_ref=basis.at[v, col],
            send_sem=col_send.at[v], recv_sem=col_recv.at[v],
            device_id={"col": 1 - col}, device_id_type=MESH,
        )

    def halo_copy(it, slot):
        axis, here = ("dom", dom) if slot < 2 else ("sub", sub)
        step = 1 if slot % 2 == 0 else -1
        return pltpu.make_async_remote_copy(
            src_ref=out_halo.at[it, slot], dst_ref=in_halo.at[it, slot],
            send_sem=halo_send.at[it, slot], recv_sem=halo_recv.at[it, slot],
            device_id={axis: here + step}, device_id_type=MESH,
        )

    def sends(slot):
        here, count = (dom, n_dom) if slot < 2 else (sub, n_sub)
        return here < count - 1 if slot % 2 == 0 else here > 0

    def receives(slot):
        here, count = (dom, n_dom) if slot < 2 else (sub, n_sub)
        return here > 0 if slot % 2 == 0 else here < count - 1

    def part(value, a):
        return value[a * width : (a + 1) * width]

    def mix_up(t, value):
        return jnp.concatenate(
            [sum(weights[t, a, b : b + 1, :] * part(value, a) for a in range(3)) for b in range(3)], axis=0
        )

    def mix_down(t, value):
        return jnp.concatenate(
            [sum(weights[t, a, b : b + 1, :] * part(value, b) for b in range(3)) for a in range(3)], axis=0
        )

    def whole(v, a):
        return jnp.concatenate([basis[v, h, a] for h in range(n_col)], axis=0)

    col_copy(0).start()

    for it in range(2):
        field = [basis[it, col, a] for a in range(3)]
        stacked = halves(jnp.concatenate(field, axis=0))
        for t in range(2):
            low = slice(inner + 2 * t * iface, inner + (2 * t + 1) * iface)
            high = slice(inner + (2 * t + 1) * iface, inner + (2 * t + 2) * iface)
            out_halo[it, 2 * t] = mix_up(t, joined(dot(stacked, pick[:, high], NN)))
            out_halo[it, 2 * t + 1] = joined(dot(stacked, pick[:, low], NN))
            for slot in (2 * t, 2 * t + 1):

                @pl.when(sends(slot))
                def _():
                    halo_copy(it, slot).start()

        if it == 0:
            lax.fori_loop(0, node // slab, build_inner, 0)
        result = [(diag_ref[a : a + 1, :] - SHIFT) * field[a] for a in range(3)]
        returned = jnp.zeros((6 * width, node), F32)
        for s in range(slots):
            span = slice(s * node, (s + 1) * node)
            near = joined(dot(stacked, pick[:, span], NN))
            back = []
            for b in range(3):
                back.append(sum(vals_ref[a, b, s : s + 1, :] * field[a] for a in range(3)))
            returned = returned + dot(halves(jnp.concatenate(back, axis=0)), pick[:, span], NT)
            for a in range(3):
                result[a] = result[a] + sum(vals_ref[a, b, s : s + 1, :] * part(near, b) for b in range(3))

        if it == 1:
            col_copy(0).wait_recv()
            col_copy(1).wait_recv()
            zero = jnp.zeros((total, node), F32)
            gram = jnp.zeros((width, 4 * total), F32)
            for a in range(3):
                r0, v1 = whole(0, a), whole(1, a)
                gram = gram + dot(basis[0, col, a], jnp.concatenate([r0, zero, zero, zero], axis=0), NT, HIGHEST)
                gram = gram + dot(field[a], jnp.concatenate([zero, r0, v1, zero], axis=0), NT, HIGHEST)

        for slot in range(4):

            @pl.when(receives(slot))
            def _():
                halo_copy(it, slot).wait_recv()

        for t in range(2):
            first = inner + 2 * t * iface
            arrived = jnp.concatenate([in_halo[it, 2 * t], mix_down(t, in_halo[it, 2 * t + 1])], axis=1)
            returned = returned + dot(halves(arrived), pick[:, first : first + 2 * iface], NT)
        returned = joined(returned)
        for a in range(3):
            result[a] = result[a] + part(returned, a)
            basis[it + 1, col, a] = result[a]
        col_copy(it + 1).start()

    for a in range(3):
        gram = gram + dot(result[a], jnp.concatenate([zero, zero, zero, whole(1, a)], axis=0), NT, HIGHEST)
    message[0] = jnp.concatenate([gram, jnp.zeros((width, 128 - 4 * total), F32)], axis=1)

    def dom_copy(k):
        return pltpu.make_async_remote_copy(
            src_ref=message.at[0], dst_ref=stage_dom.at[dom],
            send_sem=dom_send.at[k], recv_sem=dom_recv.at[k],
            device_id={"dom": lax.rem(dom + k, n_dom)}, device_id_type=MESH,
        )

    def rest_copy(k):
        peer = lax.rem(rest + k, n_rest)
        return pltpu.make_async_remote_copy(
            src_ref=message.at[1], dst_ref=stage_rest.at[rest],
            send_sem=rest_send.at[k], recv_sem=rest_recv.at[k],
            device_id={"sub": lax.div(peer, n_col), "col": lax.rem(peer, n_col)}, device_id_type=MESH,
        )

    for k in range(1, n_dom):
        dom_copy(k).start()
    stage_dom[dom] = message[0]
    for k in range(1, n_dom):
        dom_copy(k).wait_recv()
    message[1] = sum(stage_dom[i] for i in range(n_dom))
    for k in range(1, n_rest):
        rest_copy(k).start()
    stage_rest[rest] = message[1]
    for k in range(1, n_rest):
        rest_copy(k).wait_recv()
    grams = jnp.concatenate(
        [sum(stage_rest[s * n_col + h] for s in range(n_sub)) for h in range(n_col)], axis=0
    )

    s0 = grams[:, : 2 * total]
    s1 = grams[:, total : 3 * total]
    s2 = grams[:, 2 * total : 4 * total]
    norms = s0[:, :total]
    curvature = s1[:, :total] + SHIFT * norms
    big = jnp.concatenate([s0, s1], axis=0)
    stiff = SHIFT * big + jnp.concatenate([s1, s2], axis=0)
    eye = jnp.where(
        lax.broadcasted_iota(jnp.int32, (total, total), 0) == lax.broadcasted_iota(jnp.int32, (total, total), 1), 1.0, 0.0
    )
    alpha0 = eliminate(curvature, norms)
    norms_inverse = eliminate(norms, eye)
    start = eye - SHIFT * alpha0
    mixed = jnp.concatenate([start, -alpha0], axis=0)
    fresh = dot(mixed, dot(big, mixed, NN, HIGHEST), TN, HIGHEST)
    beta = dot(norms_inverse, fresh, NN, HIGHEST)
    direction = jnp.concatenate([start + beta, -alpha0], axis=0)
    curvature = dot(direction, dot(stiff, direction, NN, HIGHEST), TN, HIGHEST)
    alpha1 = eliminate(curvature, fresh)
    moved = dot(direction, alpha1, NN, HIGHEST)
    p_move, q_move = moved[:total], moved[total:]
    nothing = jnp.zeros((total, total), F32)
    sol_mix = jnp.concatenate([alpha0 + p_move, q_move, nothing], axis=0)
    res_mix = jnp.concatenate([start - SHIFT * p_move, -alpha0 - p_move - SHIFT * q_move, -q_move], axis=0)
    both = jnp.concatenate([sol_mix, res_mix], axis=1)

    col_copy(2).wait_recv()
    for a in range(3):
        every = jnp.concatenate([whole(0, a), whole(1, a), whole(2, a)], axis=0)
        answer = dot(both, every, TN, HIGHEST)
        sol_ref[a] = jnp.where(col == 0, answer[:width], answer[width:total])
        res_ref[a] = jnp.where(col == 0, answer[total : total + width], answer[total + width :])

    for v in range(3):
        col_copy(v).wait_send()
    for it in range(2):
        for slot in range(4):

            @pl.when(sends(slot))
            def _():
                halo_copy(it, slot).wait_send()

    for k in range(1, n_dom):
        dom_copy(k).wait_send()
    for k in range(1, n_rest):
        rest_copy(k).wait_send()


def body(n_dom, n_sub, n_col, rhs, diagonal, lower_vals, lower_cols, face_nodes, couple, face_count):
    shape = rhs.shape[2:]
    _, width, node = shape
    slots = lower_cols.shape[2]
    iface = face_nodes.shape[3]
    vmem = pl.BlockSpec(memory_space=pltpu.VMEM)
    dma = pltpu.SemaphoreType.DMA
    sol, res = pl.pallas_call(
        functools.partial(kernel, n_dom, n_sub, n_col),
        out_shape=[jax.ShapeDtypeStruct(shape, F32)] * 2,
        in_specs=[vmem] * 6 + [pl.BlockSpec(memory_space=pltpu.SMEM)],
        out_specs=[vmem] * 2,
        scratch_shapes=[
            pltpu.VMEM((node, slots * node + 4 * iface), jnp.bfloat16),
            pltpu.VMEM((3, n_col, 3, width, node), F32),
            pltpu.VMEM((2, 4, 3 * width, iface), F32),
            pltpu.VMEM((2, 4, 3 * width, iface), F32),
            pltpu.VMEM((2, 3, 3, iface), F32),
            pltpu.VMEM((2, width, 128), F32),
            pltpu.VMEM((n_dom, width, 128), F32),
            pltpu.VMEM((n_sub * n_col, width, 128), F32),
            dma((2, 4)),
            dma((2, 4)),
            dma((3,)),
            dma((3,)),
            dma((n_dom,)),
            dma((n_dom,)),
            dma((n_sub * n_col,)),
            dma((n_sub * n_col,)),
        ],
        compiler_params=pltpu.CompilerParams(
            collective_id=0, has_side_effects=True, vmem_limit_bytes=48 * 1024 * 1024
        ),
    )(rhs[0, 0], diagonal[0, 0], lower_vals[0, 0], lower_cols[0, 0], face_nodes[0, 0], couple[0, 0], face_count[0, 0])
    return sol[None, None], res[None, None]


def solution(mesh):
    field = P(("groups", "dom"), "sub", None, "col", None)
    placed = (
        field,
        P("dom", "sub", None, None),
        P("dom", "sub", None, None, None, None),
        P("dom", "sub", None, None),
        P("dom", "sub", None, None),
        P("dom", "sub", None, None, None, None),
        P("dom", "sub", None),
    )
    return jax.shard_map(
        functools.partial(body, mesh.shape["dom"], mesh.shape["sub"], mesh.shape["col"]),
        mesh=mesh,
        in_specs=placed,
        out_specs=(field, field),
        check_vma=False,
    )
```

time: 1670 us -> 27.2 us (0.02); the launches traced: 1640 us -> 26.9 us
  other arithmetic: 1080 us -> 0 us
  local copies, waits for them, and re-layouts: 253 us -> 4.25 us
  blocking collectives: 132 us -> 0 us
  matrix products: 83.1 us -> 0 us
  between operations: 68.7 us -> 0.69 us
  Pallas kernels: 0 us -> 22 us
  starting transfers between devices: 17.8 us -> 0 us
    div x53 -> x0, other arithmetic: 799 us -> none  [the longest x6 448 us: cholesky_solve(): middle.append(value / factor[j, j])]
    scatter-add x8 -> x0, other arithmetic: 147 us -> none  [the longest x2 43.3 us: body(): result = result.at[:, :, faces[0]].add(shifted(sent, 'dom', 1))]
    gather x15 -> x0, local copies, waits for them, and re-layouts: 142 us -> none  [the longest x3 70.8 us: local_apply(): returned = jnp.take_along_axis(back, inverse[None, None, :, :], axis=3)]
    psum x3 -> x0, blocking collectives: 124 us -> none  [the longest x1 63.8 us: body(): norms = lax.psum(gram_block(whole_start, start), ('dom', 'sub', 'col'))]
    another operation x3 -> x0, other arithmetic: 84.6 us -> none  [cholesky_solve(): return jnp.stack(answer, axis=0)]
    dot_general x21 -> x0, matrix products: 83.1 us -> none  [the longest x2 28.9 us: local_apply(): jnp.einsum('abkn,bckn->acn', blocks, near, precision=highest)]
    reduce_sum x83 -> x0, other arithmetic: 48.1 us -> none  [the longest x42 26.9 us: cholesky_solve(): pivot = jnp.sqrt(matrix[j, j] - jnp.sum(factor[j, :j] * factor[j, :j]))]
    transpose x2 -> x0, local copies, waits for them, and re-layouts: 33.1 us -> none  [local_apply(): back = jnp.einsum('abkn,acn->bckn', blocks, field, precision=highest)]
  transfers between devices with their start and end apart: 8 -> 0, of which waited for: 1 -> 0; matrix products, arithmetic and copies ran while one was open for 16% -> 0% of each run, Pallas kernels for 0% -> 0%
where the time goes in v1:
time: 27.2 us; the launch traced here: 26.9 us
  Pallas kernels  22 us (81%)
  local copies, waits for them, and re-layouts  4.25 us (16%)
  between operations  0.69 us (3%)
    pallas_call x1, Pallas kernels, body(): pl.pallas_call(functools.partial(kernel, n_dom, n_sub, n_col), out_shape=...  22 us
    unnamed x16, local copies, waits for them, and re-layouts  4.25 us

profile of v1, /device:TPU:0, one launch (start us, length us, event | category | flops | bytes accessed | tf_op | source)
XLA Modules:
  0.0 26.9 jit_solution(923384223771005707)
XLA Ops:
  0.6 0.0 copy-start.4
  0.6 0.7 %copy.20 = f32[1,1,3,512]{3,2,1,0:T(4,128)S(1)} copy(f32[1,1,3,512]{3,1,2,0:T(1,128)} %param.8) | data formatting | bytes 12288
  1.3 0.0 copy-start.3
  1.3 0.0 copy-done.4
  1.4 0.7 %copy-done.3 = f32[1,1,2,3,3,256]{5,2,4,3,1,0:T(2,128)S(1)} copy-done((f32[1,1,2,3,3,256]{5,2,4,3,1,0:T(2,128)S(1)}, f32[1,1,2,3,3,256]{5,2,4,3,1,0:T(2,128)}, u32[]{:S(2)}) %copy-start.3) | copy-done | bytes 18456
  2.1 0.0 copy-start
  2.1 0.0 copy-start.1
  2.1 0.9 %copy.17 = f32[1,1,3,3,7,512]{5,4,1,3,2,0:T(8,128)S(1)} copy(f32[1,1,3,3,7,512]{5,1,4,3,2,0:T(1,128)} %param.9) | data formatting | bytes 258048
  3.0 0.0 copy-start.2
  3.0 0.0 copy-done
  3.1 0.0 copy-done.1
  3.1 0.6 %copy-done.2 = s32[1,1,2]{2,1,0:T(1,128)S(1)} copy-done((s32[1,1,2]{2,1,0:T(1,128)S(1)}, s32[1,1,2]{2,1,0:T(1,128)}, u32[]{:S(2)}) %copy-start.2) | copy-done | bytes 32
  3.7 22.0 %shard_map.86 = (f32[3,8,512]{2,1,0:T(8,128)S(1)}, f32[3,8,512]{2,1,0:T(8,128)S(1)}) custom-call(f32[3,8,512]{2,1,0:T(8,128)S(1)} %bitcast.22, f32[3,512]{1,0:T(4,128)S(1)} %bitcast.23, f32[3,3,7,512]{3,2,1,0:T(8,128)S(1)} %bitcast.17, s32[7,512]{1,0:T(8,128)S(1)} %bitcast.19, s32[4,256]{1,0:T(4,128)S(1)} %bitcast.24, f32[2,3,3,256]{3,2,1,0:T(4,128)S(1)} %bitcast.18, ...), custom_call_target="tpu_custom_call" | custom-call | tf_op jit(solution)/shard_map/pallas_call | solution.py:302
  25.7 0.6 %copy.23 = f32[1,1,3,8,512]{4,3,2,1,0:T(8,128)} copy(f32[1,1,3,8,512]{4,3,2,1,0:T(8,128)S(1)} %bitcast.21) | data formatting | bytes 98304
  26.3 0.6 %copy.24 = f32[1,1,3,8,512]{4,3,2,1,0:T(8,128)} copy(f32[1,1,3,8,512]{4,3,2,1,0:T(8,128)S(1)} %bitcast.20) | data formatting | bytes 98304
  (2 shorter events, 0.0 us)
Async XLA Ops:
  0.6 0.7 %copy-start.4 = (s32[1,1,7,512]{3,1,2,0:T(1,128)S(1)}, s32[1,1,7,512]{3,1,2,0:T(1,128)}, u32[]{:S(2)}) copy-start(s32[1,1,7,512]{3,1,2,0:T(1,128)} %param.10) | copy-start | bytes 43012
  1.3 0.7 %copy-start.3 = (f32[1,1,2,3,3,256]{5,2,4,3,1,0:T(2,128)S(1)}, f32[1,1,2,3,3,256]{5,2,4,3,1,0:T(2,128)}, u32[]{:S(2)}) copy-start(f32[1,1,2,3,3,256]{5,2,4,3,1,0:T(2,128)} %param.12) | copy-start | bytes 55300
  2.1 1.0 %copy-start = (f32[1,1,3,8,512]{4,3,2,1,0:T(8,128)S(1)}, f32[1,1,3,8,512]{4,3,2,1,0:T(8,128)}, u32[]{:S(2)}) copy-start(f32[1,1,3,8,512]{4,3,2,1,0:T(8,128)} %param.7) | copy-start | bytes 147460
  2.1 1.0 %copy-start.1 = (s32[1,1,4,256]{3,2,1,0:T(4,128)S(1)}, s32[1,1,4,256]{3,2,1,0:T(4,128)}, u32[]{:S(2)}) copy-start(s32[1,1,4,256]{3,2,1,0:T(4,128)} %param.11) | copy-start | bytes 12292
  3.0 0.7 %copy-start.2 = (s32[1,1,2]{2,1,0:T(1,128)S(1)}, s32[1,1,2]{2,1,0:T(1,128)}, u32[]{:S(2)}) copy-start(s32[1,1,2]{2,1,0:T(1,128)} %param.13) | copy-start | bytes 28

commit v2 on v1

--- a/solution.py
+++ b/solution.py
@@ -50,31 +50,59 @@
 
 def kernel(
     n_dom, n_sub, n_col,
-    rhs_ref, diag_ref, vals_ref, cols_ref, faces_ref, couple_ref, count_ref,
-    sol_ref, res_ref,
-    pick, basis, out_halo, in_halo, weights, message, stage_dom, stage_rest,
-    halo_send, halo_recv, col_send, col_recv, dom_send, dom_recv, rest_send, rest_recv,
+    rhs_hbm, diag_hbm, vals_hbm, cols_hbm, faces_hbm, couple_hbm, count_hbm,
+    out_ref,
+    diag_ref, vals_ref, cols_ref, faces_ref, couple_ref, count_ref, load_sem,
+    pick, basis, out_halo, in_halo, weights, message, stage,
+    halo_send, halo_recv, col_send, col_recv, gram_send, gram_recv,
 ):
     dom = lax.axis_index("dom")
     sub = lax.axis_index("sub")
     col = lax.axis_index("col")
-    width = rhs_ref.shape[1]
-    node = rhs_ref.shape[2]
-    slots = cols_ref.shape[0]
-    iface = faces_ref.shape[1]
+    width = rhs_hbm.shape[1]
+    node = rhs_hbm.shape[2]
+    slots = cols_hbm.shape[0]
+    iface = faces_hbm.shape[1]
     inner = slots * node
     total = width * n_col
-    rest = sub * n_col + col
-    n_rest = n_sub * n_col
+    n_all = n_dom * n_sub * n_col
+    me = (dom * n_sub + sub) * n_col + col
+
+    def place(k):
+        peer = lax.rem(me + k, n_all)
+        return {
+            "dom": lax.div(peer, n_sub * n_col),
+            "sub": lax.rem(lax.div(peer, n_col), n_sub),
+            "col": lax.rem(peer, n_col),
+        }
+
+    def every_peer(act):
+        if n_all <= 32:
+            for k in range(1, n_all):
+                act(k)
+        else:
+            lax.fori_loop(1, n_all, lambda k, _: (act(k), 0)[1], 0)
+
+    def gram_copy(k):
+        return pltpu.make_async_remote_copy(
+            src_ref=message, dst_ref=stage.at[me], send_sem=gram_send.at[k], recv_sem=gram_recv.at[k],
+            device_id=place(k), device_id_type=MESH,
+        )
 
     barrier = pltpu.get_barrier_semaphore()
-    for k in range(1, n_dom):
-        pl.semaphore_signal(barrier, inc=1, device_id={"dom": lax.rem(dom + k, n_dom)}, device_id_type=MESH)
-    for k in range(1, n_rest):
-        peer = lax.rem(rest + k, n_rest)
-        pl.semaphore_signal(
-            barrier, inc=1, device_id={"sub": lax.div(peer, n_col), "col": lax.rem(peer, n_col)}, device_id_type=MESH
-        )
+    every_peer(lambda k: pl.semaphore_signal(barrier, inc=1, device_id=place(k), device_id_type=MESH))
+
+    loads = [
+        pltpu.make_async_copy(source, target, load_sem.at[i])
+        for i, (source, target) in enumerate(
+            [
+                (faces_hbm, faces_ref), (rhs_hbm, basis.at[0, col]), (couple_hbm, couple_ref), (count_hbm, count_ref),
+                (cols_hbm, cols_ref), (vals_hbm, vals_ref), (diag_hbm, diag_ref),
+            ]
+        )
+    ]
+    for load in loads:
+        load.start()
 
     slab = 32
 
@@ -90,17 +118,20 @@
         rows = pl.ds(pl.multiple_of(i * slab, slab), slab)
         ids = lax.broadcasted_iota(jnp.int32, (slab, node), 0) + i * slab
         for s in range(slots):
-            hit = ids == cols_ref[s : s + 1, :]
+            hit = ids == cols_ref[s]
             pick[rows, s * node : (s + 1) * node] = jnp.where(hit, 1.0, 0.0).astype(jnp.bfloat16)
         return 0
 
+    loads[0].wait()
     lax.fori_loop(0, node // slab, build_faces, 0)
-    lane = lax.broadcasted_iota(jnp.int32, (3, iface), 1)
+    for load in loads[1:4]:
+        load.wait()
+    lane = lax.broadcasted_iota(jnp.int32, (1, iface), 1)
     for t in range(2):
         for a in range(3):
-            weights[t, a] = jnp.where(lane < count_ref[t], couple_ref[t, a], 0.0)
-
-    basis[0, col] = rhs_ref[...]
+            for b in range(3):
+                weights[t, a, b] = jnp.where(lane < count_ref[t], couple_ref[a, b, t : t + 1, :], 0.0)
+
     for t in range(2):
         for it in range(2):
 
@@ -112,7 +143,7 @@
             def _():
                 in_halo[it, 2 * t + 1] = jnp.zeros((3 * width, iface), F32)
 
-    pl.semaphore_wait(barrier, n_dom - 1 + n_rest - 1)
+    pl.semaphore_wait(barrier, n_all - 1)
 
     def col_copy(v):
         return pltpu.make_async_remote_copy(
@@ -143,16 +174,21 @@
 
     def mix_up(t, value):
         return jnp.concatenate(
-            [sum(weights[t, a, b : b + 1, :] * part(value, a) for a in range(3)) for b in range(3)], axis=0
+            [sum(weights[t, a, b] * part(value, a) for a in range(3)) for b in range(3)], axis=0
         )
 
     def mix_down(t, value):
         return jnp.concatenate(
-            [sum(weights[t, a, b : b + 1, :] * part(value, b) for b in range(3)) for a in range(3)], axis=0
+            [sum(weights[t, a, b] * part(value, b) for b in range(3)) for a in range(3)], axis=0
         )
 
     def whole(v, a):
         return jnp.concatenate([basis[v, h, a] for h in range(n_col)], axis=0)
+
+    def products(left, right):
+        full = joined(sum(dot(left[a], right[a], NT) for a in range(3)))
+        half = full.shape[1] // 2
+        return full[:, :half] + full[:, half:]
 
     col_copy(0).start()
 
@@ -171,28 +207,27 @@
                     halo_copy(it, slot).start()
 
         if it == 0:
+            for load in loads[4:]:
+                load.wait()
             lax.fori_loop(0, node // slab, build_inner, 0)
-        result = [(diag_ref[a : a + 1, :] - SHIFT) * field[a] for a in range(3)]
+        result = [(diag_ref[a] - SHIFT) * field[a] for a in range(3)]
         returned = jnp.zeros((6 * width, node), F32)
         for s in range(slots):
             span = slice(s * node, (s + 1) * node)
             near = joined(dot(stacked, pick[:, span], NN))
             back = []
             for b in range(3):
-                back.append(sum(vals_ref[a, b, s : s + 1, :] * field[a] for a in range(3)))
+                back.append(sum(vals_ref[a, b, s] * field[a] for a in range(3)))
             returned = returned + dot(halves(jnp.concatenate(back, axis=0)), pick[:, span], NT)
             for a in range(3):
-                result[a] = result[a] + sum(vals_ref[a, b, s : s + 1, :] * part(near, b) for b in range(3))
+                result[a] = result[a] + sum(vals_ref[a, b, s] * part(near, b) for b in range(3))
 
         if it == 1:
             col_copy(0).wait_recv()
             col_copy(1).wait_recv()
-            zero = jnp.zeros((total, node), F32)
-            gram = jnp.zeros((width, 4 * total), F32)
-            for a in range(3):
-                r0, v1 = whole(0, a), whole(1, a)
-                gram = gram + dot(basis[0, col, a], jnp.concatenate([r0, zero, zero, zero], axis=0), NT, HIGHEST)
-                gram = gram + dot(field[a], jnp.concatenate([zero, r0, v1, zero], axis=0), NT, HIGHEST)
+            own = [halves(jnp.concatenate([basis[0, col, a], field[a]], axis=0)) for a in range(3)]
+            both = [halves(jnp.concatenate([whole(0, a), whole(1, a)], axis=0)) for a in range(3)]
+            early = products(own, both)
 
         for slot in range(4):
 
@@ -210,38 +245,16 @@
             basis[it + 1, col, a] = result[a]
         col_copy(it + 1).start()
 
-    for a in range(3):
-        gram = gram + dot(result[a], jnp.concatenate([zero, zero, zero, whole(1, a)], axis=0), NT, HIGHEST)
-    message[0] = jnp.concatenate([gram, jnp.zeros((width, 128 - 4 * total), F32)], axis=1)
-
-    def dom_copy(k):
-        return pltpu.make_async_remote_copy(
-            src_ref=message.at[0], dst_ref=stage_dom.at[dom],
-            send_sem=dom_send.at[k], recv_sem=dom_recv.at[k],
-            device_id={"dom": lax.rem(dom + k, n_dom)}, device_id_type=MESH,
-        )
-
-    def rest_copy(k):
-        peer = lax.rem(rest + k, n_rest)
-        return pltpu.make_async_remote_copy(
-            src_ref=message.at[1], dst_ref=stage_rest.at[rest],
-            send_sem=rest_send.at[k], recv_sem=rest_recv.at[k],
-            device_id={"sub": lax.div(peer, n_col), "col": lax.rem(peer, n_col)}, device_id_type=MESH,
-        )
-
-    for k in range(1, n_dom):
-        dom_copy(k).start()
-    stage_dom[dom] = message[0]
-    for k in range(1, n_dom):
-        dom_copy(k).wait_recv()
-    message[1] = sum(stage_dom[i] for i in range(n_dom))
-    for k in range(1, n_rest):
-        rest_copy(k).start()
-    stage_rest[rest] = message[1]
-    for k in range(1, n_rest):
-        rest_copy(k).wait_recv()
+    last = products([halves(result[a]) for a in range(3)], both)
+    message[...] = jnp.concatenate(
+        [early[:width, :total], early[width:], last[:, total:], jnp.zeros((width, 128 - 4 * total), F32)], axis=1
+    )
+
+    stage[me] = message[...]
+    every_peer(lambda k: gram_copy(k).start())
+    every_peer(lambda k: gram_copy(k).wait_recv())
     grams = jnp.concatenate(
-        [sum(stage_rest[s * n_col + h] for s in range(n_sub)) for h in range(n_col)], axis=0
+        [sum(stage[i * n_col + h] for i in range(n_dom * n_sub)) for h in range(n_col)], axis=0
     )
 
     s0 = grams[:, : 2 * total]
@@ -268,14 +281,15 @@
     nothing = jnp.zeros((total, total), F32)
     sol_mix = jnp.concatenate([alpha0 + p_move, q_move, nothing], axis=0)
     res_mix = jnp.concatenate([start - SHIFT * p_move, -alpha0 - p_move - SHIFT * q_move, -q_move], axis=0)
-    both = jnp.concatenate([sol_mix, res_mix], axis=1)
+    parts = halves(jnp.concatenate([sol_mix, res_mix], axis=1).T)
+    final = jnp.concatenate([parts, parts], axis=1)
 
     col_copy(2).wait_recv()
     for a in range(3):
-        every = jnp.concatenate([whole(0, a), whole(1, a), whole(2, a)], axis=0)
-        answer = dot(both, every, TN, HIGHEST)
-        sol_ref[a] = jnp.where(col == 0, answer[:width], answer[width:total])
-        res_ref[a] = jnp.where(col == 0, answer[total : total + width], answer[total + width :])
+        every = halves(jnp.concatenate([whole(0, a), whole(1, a), whole(2, a)], axis=0))
+        answer = joined(dot(final, every, NN))
+        out_ref[0, a] = jnp.where(col == 0, answer[:width], answer[width:total])
+        out_ref[1, a] = jnp.where(col == 0, answer[total : total + width], answer[total + width :])
 
     for v in range(3):
         col_copy(v).wait_send()
@@ -286,10 +300,7 @@
             def _():
                 halo_copy(it, slot).wait_send()
 
-    for k in range(1, n_dom):
-        dom_copy(k).wait_send()
-    for k in range(1, n_rest):
-        rest_copy(k).wait_send()
+    every_peer(lambda k: gram_copy(k).wait_send())
 
 
 def body(n_dom, n_sub, n_col, rhs, diagonal, lower_vals, lower_cols, face_nodes, couple, face_count):
@@ -299,34 +310,41 @@
     iface = face_nodes.shape[3]
     vmem = pl.BlockSpec(memory_space=pltpu.VMEM)
     dma = pltpu.SemaphoreType.DMA
-    sol, res = pl.pallas_call(
+    out = pl.pallas_call(
         functools.partial(kernel, n_dom, n_sub, n_col),
-        out_shape=[jax.ShapeDtypeStruct(shape, F32)] * 2,
-        in_specs=[vmem] * 6 + [pl.BlockSpec(memory_space=pltpu.SMEM)],
-        out_specs=[vmem] * 2,
+        out_shape=jax.ShapeDtypeStruct((2, *shape), F32),
+        in_specs=[pl.BlockSpec(memory_space=pltpu.HBM)] * 7,
+        out_specs=vmem,
         scratch_shapes=[
+            pltpu.VMEM((3, 1, node), F32),
+            pltpu.VMEM((3, 3, slots, 1, node), F32),
+            pltpu.VMEM((slots, 1, node), jnp.int32),
+            pltpu.VMEM((4, iface), jnp.int32),
+            pltpu.VMEM((3, 3, 2, iface), F32),
+            pltpu.SMEM((2,), jnp.int32),
+            dma((7,)),
             pltpu.VMEM((node, slots * node + 4 * iface), jnp.bfloat16),
             pltpu.VMEM((3, n_col, 3, width, node), F32),
             pltpu.VMEM((2, 4, 3 * width, iface), F32),
             pltpu.VMEM((2, 4, 3 * width, iface), F32),
-            pltpu.VMEM((2, 3, 3, iface), F32),
-            pltpu.VMEM((2, width, 128), F32),
-            pltpu.VMEM((n_dom, width, 128), F32),
-            pltpu.VMEM((n_sub * n_col, width, 128), F32),
+            pltpu.VMEM((2, 3, 3, 1, iface), F32),
+            pltpu.VMEM((width, 128), F32),
+            pltpu.VMEM((n_dom * n_sub * n_col, width, 128), F32),
             dma((2, 4)),
             dma((2, 4)),
             dma((3,)),
             dma((3,)),
-            dma((n_dom,)),
-            dma((n_dom,)),
-            dma((n_sub * n_col,)),
-            dma((n_sub * n_col,)),
+            dma((n_dom * n_sub * n_col,)),
+            dma((n_dom * n_sub * n_col,)),
         ],
         compiler_params=pltpu.CompilerParams(
-            collective_id=0, has_side_effects=True, vmem_limit_bytes=48 * 1024 * 1024
+            collective_id=0, has_side_effects=True, vmem_limit_bytes=64 * 1024 * 1024
         ),
-    )(rhs[0, 0], diagonal[0, 0], lower_vals[0, 0], lower_cols[0, 0], face_nodes[0, 0], couple[0, 0], face_count[0, 0])
-    return sol[None, None], res[None, None]
+    )(
+        rhs[0, 0], diagonal[0, 0][:, None], lower_vals[0, 0][:, :, :, None], lower_cols[0, 0][:, None],
+        face_nodes[0, 0], jnp.transpose(couple[0, 0], (1, 2, 0, 3)), face_count[0, 0],
+    )
+    return out[0][None, None], out[1][None, None]
 
 
 def solution(mesh):

time: 27.2 us -> 22.4 us (0.82)
  local copies, waits for them, and re-layouts: 4.25 us -> 1.46 us
  Pallas kernels: 22 us -> 20.1 us
    unnamed x16 -> x0, local copies, waits for them, and re-layouts: 4.25 us -> none
    pallas_call x1, Pallas kernels: 22 us -> 20.1 us  [body(): pl.pallas_call(functools.partial(kernel, n_dom, n_sub, n_col), out_shape=...]
    another operation x0 -> x1, local copies, waits for them, and re-layouts: none -> 1.46 us  [body(): return (out[0][None, None], out[1][None, None])]
where the time goes in v2:
time: 22.4 us; the launch traced here: 22.2 us
  Pallas kernels  20.1 us (90%)
  local copies, waits for them, and re-layouts  1.46 us (7%)
  between operations  0.64 us (3%)
    pallas_call x1, Pallas kernels, body(): pl.pallas_call(functools.partial(kernel, n_dom, n_sub, n_col), out_shape=...  20.1 us
    another operation x1, local copies, waits for them, and re-layouts, body(): return (out[0][None, None], out[1][None, None])  1.46 us

profile of v2, /device:TPU:0, one launch (start us, length us, event | category | flops | bytes accessed | tf_op | source)
XLA Modules:
  0.0 22.2 jit_solution(18008954298150382907)
XLA Ops:
  0.6 20.1 %shard_map.86 = f32[2,3,8,512]{3,2,1,0:T(8,128)} custom-call(f32[3,8,512]{2,1,0:T(8,128)} %bitcast.14, f32[3,1,512]{2,1,0:T(1,128)} %bitcast.17, f32[3,3,7,1,512]{4,3,2,1,0:T(1,128)} %bitcast.13, s32[7,1,512]{2,1,0:T(1,128)} %bitcast.16, s32[4,256]{1,0:T(4,128)} %bitcast.18, f32[3,3,2,256]{3,2,1,0:T(2,128)} %bitcast.15, s32[2]{0:T(128)} %bitcast.19), custom_call_target="tpu_custom_call" | custom-call | tf_op jit(solution)/shard_map/pallas_call | solution.py:313
  20.7 1.5 %slice_bitcast_fusion = (f32[1,1,3,8,512]{4,3,2,1,0:T(8,128)}, f32[1,1,3,8,512]{4,3,2,1,0:T(8,128)}) fusion(f32[2,3,8,512]{3,2,1,0:T(8,128)} %shard_map.86), kind=kLoop, calls=%fused_computation | loop fusion | bytes 196608 | tf_op jit(solution)/shard_map/broadcast_in_dim;squeeze | solution.py:347

commit v3 on v2

--- a/solution.py
+++ b/solution.py
@@ -89,9 +89,6 @@
             device_id=place(k), device_id_type=MESH,
         )
 
-    barrier = pltpu.get_barrier_semaphore()
-    every_peer(lambda k: pl.semaphore_signal(barrier, inc=1, device_id=place(k), device_id_type=MESH))
-
     loads = [
         pltpu.make_async_copy(source, target, load_sem.at[i])
         for i, (source, target) in enumerate(
@@ -103,6 +100,9 @@
     ]
     for load in loads:
         load.start()
+
+    barrier = pltpu.get_barrier_semaphore()
+    every_peer(lambda k: pl.semaphore_signal(barrier, inc=1, device_id=place(k), device_id_type=MESH))
 
     slab = 32
 
@@ -143,8 +143,6 @@
             def _():
                 in_halo[it, 2 * t + 1] = jnp.zeros((3 * width, iface), F32)
 
-    pl.semaphore_wait(barrier, n_all - 1)
-
     def col_copy(v):
         return pltpu.make_async_remote_copy(
             src_ref=basis.at[v, col], dst_ref=basis.at[v, col],
@@ -190,7 +188,12 @@
         half = full.shape[1] // 2
         return full[:, :half] + full[:, half:]
 
-    col_copy(0).start()
+    def launch(it, slots_sent):
+        for slot in slots_sent:
+
+            @pl.when(sends(slot))
+            def _():
+                halo_copy(it, slot).start()
 
     for it in range(2):
         field = [basis[it, col, a] for a in range(3)]
@@ -200,12 +203,12 @@
             high = slice(inner + (2 * t + 1) * iface, inner + (2 * t + 2) * iface)
             out_halo[it, 2 * t] = mix_up(t, joined(dot(stacked, pick[:, high], NN)))
             out_halo[it, 2 * t + 1] = joined(dot(stacked, pick[:, low], NN))
-            for slot in (2 * t, 2 * t + 1):
-
-                @pl.when(sends(slot))
-                def _():
-                    halo_copy(it, slot).start()
-
+            if it == 1:
+                launch(it, (2 * t, 2 * t + 1))
+        if it == 0:
+            pl.semaphore_wait(barrier, n_all - 1)
+            launch(it, range(4))
+            col_copy(0).start()
         if it == 0:
             for load in loads[4:]:
                 load.wait()

time: 22.4 us -> 22.2 us (level)
  no operation moved by 1% of the time
where the time goes in v3:
time: 22.2 us; the launch traced here: 22 us
  Pallas kernels  19.9 us (90%)
  local copies, waits for them, and re-layouts  1.46 us (7%)
  between operations  0.64 us (3%)
    pallas_call x1, Pallas kernels, body(): pl.pallas_call(functools.partial(kernel, n_dom, n_sub, n_col), out_shape=...  19.9 us
    another operation x1, local copies, waits for them, and re-layouts, body(): return (out[0][None, None], out[1][None, None])  1.46 us

profile of v3, /device:TPU:0, one launch (start us, length us, event | category | flops | bytes accessed | tf_op | source)
XLA Modules:
  0.0 22.0 jit_solution(11404437922458219881)
XLA Ops:
  0.6 19.9 %shard_map.86 = f32[2,3,8,512]{3,2,1,0:T(8,128)} custom-call(f32[3,8,512]{2,1,0:T(8,128)} %bitcast.14, f32[3,1,512]{2,1,0:T(1,128)} %bitcast.17, f32[3,3,7,1,512]{4,3,2,1,0:T(1,128)} %bitcast.13, s32[7,1,512]{2,1,0:T(1,128)} %bitcast.16, s32[4,256]{1,0:T(4,128)} %bitcast.18, f32[3,3,2,256]{3,2,1,0:T(2,128)} %bitcast.15, s32[2]{0:T(128)} %bitcast.19), custom_call_target="tpu_custom_call" | custom-call | tf_op jit(solution)/shard_map/pallas_call | solution.py:316
  20.5 1.5 %slice_bitcast_fusion = (f32[1,1,3,8,512]{4,3,2,1,0:T(8,128)}, f32[1,1,3,8,512]{4,3,2,1,0:T(8,128)}) fusion(f32[2,3,8,512]{3,2,1,0:T(8,128)} %shard_map.86), kind=kLoop, calls=%fused_computation | loop fusion | bytes 196608 | tf_op jit(solution)/shard_map/broadcast_in_dim;squeeze | solution.py:350

commit v4 on v3

--- a/solution.py
+++ b/solution.py
@@ -54,7 +54,7 @@
     out_ref,
     diag_ref, vals_ref, cols_ref, faces_ref, couple_ref, count_ref, load_sem,
     pick, basis, out_halo, in_halo, weights, message, stage,
-    halo_send, halo_recv, col_send, col_recv, gram_send, gram_recv,
+    halo_send, halo_recv, col_send, col_recv, gram_send, gram_recv, pair_sem,
 ):
     dom = lax.axis_index("dom")
     sub = lax.axis_index("sub")
@@ -65,16 +65,12 @@
     iface = faces_hbm.shape[1]
     inner = slots * node
     total = width * n_col
-    n_all = n_dom * n_sub * n_col
-    me = (dom * n_sub + sub) * n_col + col
+    n_all = n_dom * n_sub
+    me = dom * n_sub + sub
 
     def place(k):
         peer = lax.rem(me + k, n_all)
-        return {
-            "dom": lax.div(peer, n_sub * n_col),
-            "sub": lax.rem(lax.div(peer, n_col), n_sub),
-            "col": lax.rem(peer, n_col),
-        }
+        return {"dom": lax.div(peer, n_sub), "sub": lax.rem(peer, n_sub)}
 
     def every_peer(act):
         if n_all <= 32:
@@ -101,7 +97,13 @@
     for load in loads:
         load.start()
 
+    pair_copy = pltpu.make_async_remote_copy(
+        src_ref=message.at[col], dst_ref=message.at[col], send_sem=pair_sem.at[0], recv_sem=pair_sem.at[1],
+        device_id={"col": 1 - col}, device_id_type=MESH,
+    )
+
     barrier = pltpu.get_barrier_semaphore()
+    pl.semaphore_signal(barrier, inc=1, device_id={"col": 1 - col}, device_id_type=MESH)
     every_peer(lambda k: pl.semaphore_signal(barrier, inc=1, device_id=place(k), device_id_type=MESH))
 
     slab = 32
@@ -206,7 +208,7 @@
             if it == 1:
                 launch(it, (2 * t, 2 * t + 1))
         if it == 0:
-            pl.semaphore_wait(barrier, n_all - 1)
+            pl.semaphore_wait(barrier, n_all)
             launch(it, range(4))
             col_copy(0).start()
         if it == 0:
@@ -246,18 +248,22 @@
         for a in range(3):
             result[a] = result[a] + part(returned, a)
             basis[it + 1, col, a] = result[a]
-        col_copy(it + 1).start()
+        if it == 0:
+            col_copy(1).start()
 
     last = products([halves(result[a]) for a in range(3)], both)
-    message[...] = jnp.concatenate(
+    message[col] = jnp.concatenate(
         [early[:width, :total], early[width:], last[:, total:], jnp.zeros((width, 128 - 4 * total), F32)], axis=1
     )
 
+    pair_copy.start()
+    col_copy(2).start()
+    pair_copy.wait_recv()
+    every_peer(lambda k: gram_copy(k).start())
     stage[me] = message[...]
-    every_peer(lambda k: gram_copy(k).start())
     every_peer(lambda k: gram_copy(k).wait_recv())
     grams = jnp.concatenate(
-        [sum(stage[i * n_col + h] for i in range(n_dom * n_sub)) for h in range(n_col)], axis=0
+        [sum(stage[i, h] for i in range(n_all)) for h in range(n_col)], axis=0
     )
 
     s0 = grams[:, : 2 * total]
@@ -303,6 +309,7 @@
             def _():
                 halo_copy(it, slot).wait_send()
 
+    pair_copy.wait_send()
     every_peer(lambda k: gram_copy(k).wait_send())
 
 
@@ -331,14 +338,15 @@
             pltpu.VMEM((2, 4, 3 * width, iface), F32),
             pltpu.VMEM((2, 4, 3 * width, iface), F32),
             pltpu.VMEM((2, 3, 3, 1, iface), F32),
-            pltpu.VMEM((width, 128), F32),
-            pltpu.VMEM((n_dom * n_sub * n_col, width, 128), F32),
+            pltpu.VMEM((n_col, width, 128), F32),
+            pltpu.VMEM((n_dom * n_sub, n_col, width, 128), F32),
             dma((2, 4)),
             dma((2, 4)),
             dma((3,)),
             dma((3,)),
-            dma((n_dom * n_sub * n_col,)),
-            dma((n_dom * n_sub * n_col,)),
+            dma((n_dom * n_sub,)),
+            dma((n_dom * n_sub,)),
+            dma((2,)),
         ],
         compiler_params=pltpu.CompilerParams(
             collective_id=0, has_side_effects=True, vmem_limit_bytes=64 * 1024 * 1024

time: 22.2 us -> 22 us (level)
  no operation moved by 1% of the time
where the time goes in v4:
time: 22 us; the launch traced here: 21.8 us
  Pallas kernels  19.7 us (90%)
  local copies, waits for them, and re-layouts  1.46 us (7%)
  between operations  0.64 us (3%)
    pallas_call x1, Pallas kernels, body(): pl.pallas_call(functools.partial(kernel, n_dom, n_sub, n_col), out_shape=...  19.7 us
    another operation x1, local copies, waits for them, and re-layouts, body(): return (out[0][None, None], out[1][None, None])  1.46 us

profile of v4, /device:TPU:0, one launch (start us, length us, event | category | flops | bytes accessed | tf_op | source)
XLA Modules:
  0.0 21.8 jit_solution(6810349915587163447)
XLA Ops:
  0.6 19.7 %shard_map.86 = f32[2,3,8,512]{3,2,1,0:T(8,128)} custom-call(f32[3,8,512]{2,1,0:T(8,128)} %bitcast.14, f32[3,1,512]{2,1,0:T(1,128)} %bitcast.17, f32[3,3,7,1,512]{4,3,2,1,0:T(1,128)} %bitcast.13, s32[7,1,512]{2,1,0:T(1,128)} %bitcast.16, s32[4,256]{1,0:T(4,128)} %bitcast.18, f32[3,3,2,256]{3,2,1,0:T(2,128)} %bitcast.15, s32[2]{0:T(128)} %bitcast.19), custom_call_target="tpu_custom_call" | custom-call | tf_op jit(solution)/shard_map/pallas_call | solution.py:323
  20.3 1.5 %slice_bitcast_fusion = (f32[1,1,3,8,512]{4,3,2,1,0:T(8,128)}, f32[1,1,3,8,512]{4,3,2,1,0:T(8,128)}) fusion(f32[2,3,8,512]{3,2,1,0:T(8,128)} %shard_map.86), kind=kLoop, calls=%fused_computation | loop fusion | bytes 196608 | tf_op jit(solution)/shard_map/broadcast_in_dim;squeeze | solution.py:358
